TPU v7x, 512 devices: a whole 4x8x8 slice. The times are simulated.
512 devices in a mesh: shot: 8 (over z_lo, core), space: 64 (over y, z_hi, x).
Axes of the slice: x: 4, y: 8, z: 8 (z_hi: 2, z_lo: 4; z = z_hi * 4 + z_lo), core: 2. Of those that a mesh axis runs over, the one named last changes fastest.
Arguments:
- velocity_term: float32 [512, 64, 128], P('space'), may hold values from 0.05 to 0.2
- forward_previous: float32 [8, 512, 64, 128], P('shot', 'space'), may hold values from -6 to 6
- forward_current: float32 [8, 512, 64, 128], P('shot', 'space'), may hold values from -6 to 6
- adjoint_previous: float32 [8, 512, 64, 128], P('shot', 'space'), may hold values from -6 to 6
- adjoint_current: float32 [8, 512, 64, 128], P('shot', 'space'), may hold values from -6 to 6
- source_cell: int32 [8], P('shot'), may hold values from 0 to 4194303
- wavelet: float32 [8, 2], P('shot'), may hold values from -40 to 40
- trace_cells: int32 [8, 512, 8], P('shot'), may hold values from 0 to 4194303, as said below
- trace_weights: float32 [8, 512, 8], P('shot'), may hold values from -2 to 2
- observed: float32 [8, 2, 512], P('shot', None, 'space'), may hold values from -6 to 6
Outputs:
- forward_next: float32 [8, 512, 64, 128], P('shot', 'space')
- adjoint_next: float32 [8, 512, 64, 128], P('shot', 'space')
- residual: float32 [8, 2, 512], P('shot', None, 'space')
- gradient: float32 [512, 64, 128], P('space', 'shot')
Inputs may be any that keep to these rules, and one draw needn't show every extreme that they name: `trace_cells`: each trace's footprint is 8 cells in a row along the first dimension at one position of the other two; a trace lies in the first quarter of the first dimension with chance about one half.
All inputs are finite; a program needn't handle non-finite values.
Results may differ from a plain program's by a relative error of at most 0.0001.
Values sent between devices are 32-bit elements; how exact they have to be, the bound alone decides.
A program may use at most 64 MiB of HBM per device.

v0:
```python
import jax
import jax.numpy as jnp
from jax import lax
from jax.sharding import PartitionSpec as P

coeffs = (-205.0 / 72.0, 8.0 / 5.0, -1.0 / 5.0, 8.0 / 315.0, -1.0 / 560.0)


def padded_2(cells, sides, width):
    for axis, dim in sides:
        count = lax.axis_size(axis)
        ends = count - 1
        head = lax.slice_in_dim(cells, 0, width, axis=dim)
        tail = lax.slice_in_dim(cells, cells.shape[dim] - width, cells.shape[dim], axis=dim)
        cells = jnp.concatenate(
            [
                lax.ppermute(tail, axis, [(i, (i + 1) % count) for i in range(ends)]),
                cells,
                lax.ppermute(head, axis, [((i + 1) % count, i) for i in range(ends)]),
            ],
            axis=dim,
        )
    return cells


def laplace_ext(field):
    count = field.shape[0] - 8
    core = field[4 : 4 + count]
    width_y = core.shape[1]
    width_z = core.shape[2]
    padded = jnp.pad(core, ((0, 0), (4, 4), (4, 4)))
    result = 3.0 * coeffs[0] * core
    for j in range(1, 5):
        along_x = field[4 + j : 4 + j + count] + field[4 - j : 4 - j + count]
        along_y = (
            padded[:, 4 + j : 4 + j + width_y, 4 : 4 + width_z]
            + padded[:, 4 - j : 4 - j + width_y, 4 : 4 + width_z]
        )
        along_z = (
            padded[:, 4 : 4 + width_y, 4 + j : 4 + j + width_z]
            + padded[:, 4 : 4 + width_y, 4 - j : 4 - j + width_z]
        )
        result = result + coeffs[j] * (along_x + along_y + along_z)
    return result


def per_device(
    velocity_term,
    forward_previous,
    forward_current,
    adjoint_previous,
    adjoint_current,
    source_cell,
    wavelet,
    trace_cells,
    trace_weights,
    observed,
):
    slab_x, width_y, width_z = velocity_term.shape
    plane = width_y * width_z
    anchor = lax.axis_index("space") * slab_x
    weights = trace_weights[0]

    def add_at(field, speed, start_x, cells, amounts):
        count = field.shape[0] * plane
        local = cells - start_x * plane
        inside = (local >= 0) & (local < count)
        clipped = jnp.clip(local, 0, count - 1)
        adds = jnp.where(inside, speed.reshape(-1)[clipped] * amounts, 0.0)
        flat = field.reshape(-1).at[clipped.reshape(-1)].add(adds.reshape(-1))
        return flat.reshape(field.shape)

    def add_source(field, speed, start_x, amount):
        return add_at(field, speed, start_x, source_cell[0].reshape(1), amount.reshape(1))

    def add_inject(field, speed, start_x, values):
        return add_at(field, speed, start_x, trace_cells[0], weights * values[:, None])

    own_local = trace_cells[0] - anchor * plane
    own_inside = (own_local >= 0) & (own_local < slab_x * plane)
    own_clipped = jnp.clip(own_local, 0, slab_x * plane - 1)

    def sample(field):
        return jnp.sum(
            jnp.where(own_inside, field.reshape(-1)[own_clipped] * weights, 0.0), axis=-1
        )

    p_before = forward_previous[0]
    p_now = forward_current[0]
    a_before = adjoint_previous[0]
    a_now = adjoint_current[0]
    first = padded_2(jnp.stack([p_now, a_now]), (("space", 1),), 4)
    lap_zero = laplace_ext(first[0])
    lap_adjoint = laplace_ext(first[1])
    p_one = add_source(
        2.0 * p_now - p_before + velocity_term * lap_zero, velocity_term, anchor, wavelet[0, 0]
    )
    lap_one = laplace_ext(padded_2(p_one, (("space", 0),), 4))
    p_two = add_source(
        2.0 * p_one - p_now + velocity_term * lap_one, velocity_term, anchor, wavelet[0, 1]
    )
    partials = jnp.stack([sample(p_one), sample(p_two)])
    synthetic_own = lax.psum_scatter(partials, "space", scatter_dimension=1, tiled=True)
    misfit_own = synthetic_own - observed[0]
    misfit_all = lax.all_gather(misfit_own, "space", axis=1, tiled=True)
    a_one = add_inject(
        2.0 * a_now - a_before + velocity_term * lap_adjoint, velocity_term, anchor, misfit_all[1]
    )
    lap_adj_one = laplace_ext(padded_2(a_one, (("space", 0),), 4))
    a_two = add_inject(
        2.0 * a_one - a_now + velocity_term * lap_adj_one, velocity_term, anchor, misfit_all[0]
    )
    terms = a_one * lap_one + a_two * lap_zero
    scale = 1.0 / (lax.axis_size("shot") * forward_current.shape[0])
    gradient = lax.psum_scatter(terms, "shot", scatter_dimension=1, tiled=True) * scale
    return (p_two[None], a_two[None], misfit_own[None], gradient)


def solution(mesh):
    placed = (
        P("space", None, None),
        P("shot", "space", None, None),
        P("shot", "space", None, None),
        P("shot", "space", None, None),
        P("shot", "space", None, None),
        P("shot"),
        P("shot", None),
        P("shot", None, None),
        P("shot", None, None),
        P("shot", None, "space"),
    )
    return jax.shard_map(
        per_device,
        mesh=mesh,
        in_specs=placed,
        out_specs=(
            P("shot", "space", None, None),
            P("shot", "space", None, None),
            P("shot", None, "space"),
            P("space", "shot", None),
        ),
        check_vma=False,
    )
```

profile of v0, /device:TPU:10, one launch (start us, length us, event | category | flops | bytes accessed | tf_op | source)
XLA Modules:
  0.0 707.6 jit_solution(15188208120196253433)
XLA Ops:
  7.2 1.0 constant_dynamic-update-slice_fusion.1
  8.3 3.4 collective-permute-start.1
  11.7 2.4 collective-permute-start
  15.9 0.6 compare_select_fusion.1
  17.3 0.7 squeeze.29
  18.6 40.5 %gather_fusion = f32[4096]{0:T(1024)} fusion(f32[65536]{0:T(1024)S(1)} %bitcast.176, s32[4096]{0:T(1024)S(1)} %broadcast_clamp_fusion), kind=kCustom, calls=%fused_computation | custom fusion | bytes 49152 | tf_op jit(solution)/shard_map/gather | solution.py:69
  59.1 1.3 dynamic-slice.21
  61.0 0.6 fusion.167
  61.7 1.3 fusion.154
  63.0 2.1 fusion.155
  65.1 23.0 %gather_fusion.1 = f32[4096]{0:T(1024)S(1)} fusion(f32[65536]{0:T(1024)S(1)} %fusion.155, s32[4096]{0:T(1024)S(1)} %broadcast_clamp_fusion), kind=kCustom, calls=%fused_computation.1 | custom fusion | bytes 49152 | tf_op jit(solution)/shard_map/gather | solution.py:85
  88.2 3.5 collective-permute-start.3
  91.7 10.0 %collective-permute-start.2 = (f32[4,64,128]{2,1,0:T(8,128)S(1)}, f32[4,64,128]{2,1,0:T(8,128)S(1)}, u32[]{:S(2)}, u32[]{:S(2)}) collective-permute-start(f32[4,64,128]{2,1,0:T(8,128)S(1)} %bitcast.193), channel_id=1, source_target_pairs={{1,0},{2,1},{3,2},{4,3},{5,4},{6,5},{7,6},{8,7},{9,8},{10,9},{11,1... | collective-permute-start | bytes 393224 | tf_op jit(solution)/shard_map/ppermute | solution.py:19
  102.0 0.6 fusion.55
  103.0 1.6 collective-permute-done.2
  104.7 0.6 multiply_add_fusion.1
  105.3 2.2 fusion.156
  107.5 23.0 %gather_fusion.2 = f32[4096]{0:T(1024)S(1)} fusion(f32[65536]{0:T(1024)S(1)} %fusion.156, s32[4096]{0:T(1024)S(1)} %broadcast_clamp_fusion), kind=kCustom, calls=%fused_computation.2 | custom fusion | bytes 49152 | tf_op jit(solution)/shard_map/gather | solution.py:85
  130.7 0.8 copy-done.6
  131.9 206.5 %all-reduce.4 = f32[2,512]{1,0:T(2,128)S(1)} all-reduce(f32[2,512]{1,0:T(2,128)S(1)} %pad_maximum_fusion.6), channel_id=2, replica_groups=mesh['shot'=8,'space'=64] {'space'}, use_global_device_ids=true, to_apply=%region_2.3.clone | all-reduce | flops 1024 | bytes 8192
  338.4 0.6 fusion.159
  339.1 203.5 %all-gather = f32[64,8,2]{1,2,0:T(2,128)S(1)} all-gather(f32[1,8,2]{1,2,0:T(2,128)S(1)} %get-tuple-element.57), channel_id=1, replica_groups=mesh['shot'=8,'space'=64] {'space'}, dimensions={0}, use_global_device_ids=true | all-gather | bytes 4160 | tf_op jit(solution)/shard_map/all_gather | solution.py:105
  543.9 28.0 %scatter_fusion = f32[65536]{0:T(1024)S(1)} fusion(f32[65536]{0:T(1024)S(1)} %bitcast.183, s32[4096]{0:T(1024)S(1)} %bitcast.191, f32[4096]{0:T(1024)S(1)} %get-tuple-element.55), kind=kCustom, calls=%fused_computation.3 | custom fusion | flops 4096 | bytes 65536 | tf_op jit(solution)/shard_map/scatter-add | solution.py:70
  571.9 1.9 collective-permute-start.5
  573.8 3.9 collective-permute-start.4
  577.7 1.0 collective-permute-done.5
  578.7 1.9 collective-permute-done.4
  580.7 0.6 fusion.8
  581.3 28.0 %scatter_fusion.1 = f32[65536]{0:T(1024)S(1)} fusion(f32[65536]{0:T(1024)S(1)} %bitcast.186, s32[4096]{0:T(1024)S(1)} %bitcast.192, f32[4096]{0:T(1024)S(1)} %get-tuple-element.54), kind=kCustom, calls=%fused_computation.4 | custom fusion | flops 4096 | bytes 65536 | tf_op jit(solution)/shard_map/scatter-add | solution.py:70
  609.3 0.8 multiply_add_fusion
  610.1 89.3 %reduce-scatter.3.cloned.1.call-done = f32[8,8,128]{2,1,0:T(8,128)} async-done(((f32[8,64,128]{2,1,0:T(8,128)}), f32[8,8,128]{2,1,0:T(8,128)}) %reduce-scatter.3.cloned.1.call-update) | async-done | bytes 32784 | tf_op jit(solution)/shard_map/reduce_scatter | solution.py:115
  699.4 1.4 broadcast_multiply_fusion
  (67 shorter events, 4.5 us)
Async XLA Ops:
  7.2 1.1 copy-start.7
  7.2 692.2 %reduce-scatter.3.cloned.1.call-start = ((), (), s32[]{:S(2)}) async-start(), calls=%async_computation.1 | async-start | bytes 294912 | tf_op jit(solution)/shard_map/reduce_scatter | solution.py:115
  8.3 6.5 copy-start.16
  8.3 53.3 %collective-permute-start.1 = (f32[2,4,64,128]{3,2,1,0:T(8,128)S(1)}, f32[2,4,64,128]{3,2,1,0:T(8,128)S(1)}, u32[]{:S(2)}, u32[]{:S(2)}) collective-permute-start(f32[2,4,64,128]{3,2,1,0:T(8,128)S(1)} %get-tuple-element.49), channel_id=1, source_target_pairs={{0,1},{1,2},{2,3},{3,4},{4,5},{5,6},{6,7},{7,8},{8,9},{9,10},{10,1... | collective-permute-start | bytes 786440 | tf_op jit(solution)/shard_map/ppermute | solution.py:17
  11.7 49.9 %collective-permute-start = (f32[2,4,64,128]{3,2,1,0:T(8,128)S(1)}, f32[2,4,64,128]{3,2,1,0:T(8,128)S(1)}, u32[]{:S(2)}, u32[]{:S(2)}) collective-permute-start(f32[2,4,64,128]{3,2,1,0:T(8,128)S(1)} %get-tuple-element.48), channel_id=1, source_target_pairs={{1,0},{2,1},{3,2},{4,3},{5,4},{6,5},{7,6},{8,7},{9,8},{10,9},{11,1... | collective-permute-start | bytes 786440 | tf_op jit(solution)/shard_map/ppermute | solution.py:19
  15.0 0.7 copy-start.9
  16.5 0.7 copy-start.17
  17.2 1.4 copy-start
  17.3 41.8 %copy-start.5 = (f32[1,512,8]{2,1,0:T(8,128)}, f32[1,512,8]{2,1,0:T(8,128)S(1)}, u32[]{:S(2)}) copy-start(f32[1,512,8]{2,1,0:T(8,128)S(1)} %copy.19) | copy-start | bytes 49156
  18.6 43.1 %copy-start.4 = (f32[1,8,64,128]{3,2,1,0:T(8,128)S(1)}, f32[1,8,64,128]{3,2,1,0:T(8,128)}, u32[]{:S(2)}) copy-start(f32[1,8,64,128]{3,2,1,0:T(8,128)} %param.16) | copy-start | bytes 786436
  18.6 43.1 %copy-start.12 = (f32[1,8,64,128]{3,2,1,0:T(8,128)S(1)}, f32[1,8,64,128]{3,2,1,0:T(8,128)}, u32[]{:S(2)}) copy-start(f32[1,8,64,128]{3,2,1,0:T(8,128)} %param.15) | copy-start | bytes 786436
  60.4 0.7 copy-start.18
  65.1 36.8 %copy-start.13 = (f32[1,8,64,128]{3,2,1,0:T(8,128)S(1)}, f32[1,8,64,128]{3,2,1,0:T(8,128)}, u32[]{:S(2)}) copy-start(f32[1,8,64,128]{3,2,1,0:T(8,128)} %param.17) | copy-start | bytes 786436
  88.2 13.8 %copy-start.8 = (f32[1,8,64,128]{3,2,1,0:T(8,128)S(1)}, f32[1,8,64,128]{3,2,1,0:T(8,128)}, u32[]{:S(2)}) copy-start(f32[1,8,64,128]{3,2,1,0:T(8,128)} %param.18) | copy-start | bytes 786436
  88.2 14.8 %collective-permute-start.3 = (f32[4,64,128]{2,1,0:T(8,128)S(1)}, f32[4,64,128]{2,1,0:T(8,128)S(1)}, u32[]{:S(2)}, u32[]{:S(2)}) collective-permute-start(f32[4,64,128]{2,1,0:T(8,128)S(1)} %bitcast.194), channel_id=1, source_target_pairs={{0,1},{1,2},{2,3},{3,4},{4,5},{5,6},{6,7},{7,8},{8,9},{9,10},{10,1... | collective-permute-start | bytes 393224 | tf_op jit(solution)/shard_map/ppermute | solution.py:17
  91.7 13.0 %collective-permute-start.2 = (f32[4,64,128]{2,1,0:T(8,128)S(1)}, f32[4,64,128]{2,1,0:T(8,128)S(1)}, u32[]{:S(2)}, u32[]{:S(2)}) collective-permute-start(f32[4,64,128]{2,1,0:T(8,128)S(1)} %bitcast.193), channel_id=1, source_target_pairs={{1,0},{2,1},{3,2},{4,3},{5,4},{6,5},{7,6},{8,7},{9,8},{10,9},{11,1... | collective-permute-start | bytes 393224 | tf_op jit(solution)/shard_map/ppermute | solution.py:19
  107.5 23.0 %copy-start.1 = (f32[65536]{0:T(1024)}, f32[65536]{0:T(1024)S(1)}, u32[]{:S(2)}) copy-start(f32[65536]{0:T(1024)S(1)} %fusion.156) | copy-start | bytes 786436
  107.5 23.2 %copy-start.10 = (s32[1,512,8]{2,1,0:T(8,128)S(1)}, s32[1,512,8]{2,1,0:T(8,128)}, u32[]{:S(2)}) copy-start(s32[1,512,8]{2,1,0:T(8,128)} %copy-done.9) | copy-start | bytes 49156
  130.5 1.0 copy-start.6
  130.5 413.3 %copy-start.14 = (s32[4096,1]{0,1:T(1,128)S(1)}, s32[4096,1]{0,1:T(1,128)}, u32[]{:S(2)}) copy-start(s32[4096,1]{0,1:T(1,128)} %compare_select_fusion.1) | copy-start | bytes 49156
  131.9 206.5 %copy-start.19 = (f32[1,2,8]{2,1,0:T(2,128)S(1)}, f32[1,2,8]{2,1,0:T(2,128)}, u32[]{:S(2)}) copy-start(f32[1,2,8]{2,1,0:T(2,128)} %param.23) | copy-start | bytes 196
  543.1 0.7 copy-start.3
  543.1 0.7 copy-start.15
  571.9 6.9 collective-permute-start.5
  573.8 6.9 collective-permute-start.4
  581.3 28.0 %copy-start.11 = (f32[8,64,128]{2,1,0:T(8,128)S(1)}, f32[8,64,128]{2,1,0:T(8,128)}, u32[]{:S(2)}) copy-start(f32[8,64,128]{2,1,0:T(8,128)} %get-tuple-element.47) | copy-start | bytes 786436
  609.3 0.8 copy-start.2
Sparse Core Ops, SparseCore 0:
  610.2 89.1 reduce-scatter.2
where the time goes:
time: 708 us
  blocking collectives  410 us (58%)
  local copies, waits for them, and re-layouts  94.6 us (13%)
  waiting for transfers between devices  94.4 us (13%)
  other arithmetic  67.1 us (9%)
  starting transfers between devices  25.3 us (4%)
  between operations  16.2 us (2%)
    unnamed x1, blocking collectives  207 us
    all_gather x1, blocking collectives, per_device(): misfit_all = lax.all_gather(misfit_own, 'space', axis=1, tiled=True)  204 us
    reduce_scatter x1, waiting for transfers between devices, per_device(): lax.psum_scatter(terms, 'shot', scatter_dimension=1, tiled=True) * scale  89.3 us
    scatter-add x4, other arithmetic, add_at(): flat = field.reshape(-1).at[clipped.reshape(-1)].add(adds.reshape(-1))  60.2 us
    gather x4, local copies, waits for them, and re-layouts, sample(): field.reshape(-1)[own_clipped] * weights  46.4 us
    gather x1, local copies, waits for them, and re-layouts, add_at(): adds = jnp.where(inside, speed.reshape(-1)[clipped] * amounts, 0.0)  40.5 us
    ppermute x3, starting transfers between devices, padded_2(): lax.ppermute(head, axis, [((i + 1) % count, i) for i in range(ends)])  16.4 us
  transfers between devices with their start and end apart: 7, of which 5 were waited for; matrix products, arithmetic and copies ran while one was open for 6% of the time, Pallas kernels for 0%

commit v1 on v0

--- a/solution.py
+++ b/solution.py
@@ -102,7 +102,9 @@
     partials = jnp.stack([sample(p_one), sample(p_two)])
     synthetic_own = lax.psum_scatter(partials, "space", scatter_dimension=1, tiled=True)
     misfit_own = synthetic_own - observed[0]
-    misfit_all = lax.all_gather(misfit_own, "space", axis=1, tiled=True)
+    misfit_all = jnp.concatenate(
+        lax.all_to_all(jnp.stack([misfit_own] * lax.axis_size("space")), "space", 0, 0), axis=1
+    )
     a_one = add_inject(
         2.0 * a_now - a_before + velocity_term * lap_adjoint, velocity_term, anchor, misfit_all[1]
     )

time: 708 us -> 511 us (0.72)
  the two profiles are of different devices: /device:TPU:10 before, /device:TPU:2 now
where the time goes in v1:
time: 511 us; the launch traced here: 510 us
  blocking collectives  218 us (43%)
  local copies, waits for them, and re-layouts  96.3 us (19%)
  other arithmetic  68.6 us (13%)
  waiting for transfers between devices  61.5 us (12%)
  starting transfers between devices  48.8 us (10%)
  between operations  16.4 us (3%)
    unnamed x1, blocking collectives  218 us
    scatter-add x4, other arithmetic, add_at(): flat = field.reshape(-1).at[clipped.reshape(-1)].add(adds.reshape(-1))  61.1 us
    gather x4, local copies, waits for them, and re-layouts, sample(): field.reshape(-1)[own_clipped] * weights  46.4 us
    reduce_scatter x1, waiting for transfers between devices, per_device(): lax.psum_scatter(terms, 'shot', scatter_dimension=1, tiled=True) * scale  45.4 us
    gather x1, local copies, waits for them, and re-layouts, add_at(): adds = jnp.where(inside, speed.reshape(-1)[clipped] * amounts, 0.0)  40.3 us
    all_to_all x1, starting transfers between devices, per_device(): lax.all_to_all(jnp.stack([misfit_own] * lax.axis_size('space')), 'space',...  21.5 us
    ppermute x3, starting transfers between devices, padded_2(): lax.ppermute(tail, axis, [(i, (i + 1) % count) for i in range(ends)])  16 us
    all_to_all x1, waiting for transfers between devices, per_device(): lax.all_to_all(jnp.stack([misfit_own] * lax.axis_size('space')), 'space',...  12.6 us
  transfers between devices with their start and end apart: 8, of which 5 were waited for; matrix products, arithmetic and copies ran while one was open for 13% of the time, Pallas kernels for 0%

profile of v1, /device:TPU:2, one launch (start us, length us, event | category | flops | bytes accessed | tf_op | source)
XLA Modules:
  0.0 509.9 jit_solution(3703127428159719327)
XLA Ops:
  7.2 1.0 constant_dynamic-update-slice_fusion.1
  8.3 3.4 collective-permute-start.1
  11.7 5.7 %collective-permute-start = (f32[2,4,64,128]{3,2,1,0:T(8,128)S(1)}, f32[2,4,64,128]{3,2,1,0:T(8,128)S(1)}, u32[]{:S(2)}, u32[]{:S(2)}) collective-permute-start(f32[2,4,64,128]{3,2,1,0:T(8,128)S(1)} %get-tuple-element.50), channel_id=1, source_target_pairs={{1,0},{2,1},{3,2},{4,3},{5,4},{6,5},{7,6},{8,7},{9,8},{10,9},{11,1... | collective-permute-start | bytes 786440 | tf_op jit(solution)/shard_map/ppermute | solution.py:19
  18.5 0.6 compare_select_fusion.1
  21.4 1.3 fusion.154
  22.7 2.2 fusion.155
  24.9 0.7 fusion.163
  25.6 10.3 %collective-permute-start.3 = (f32[4,64,128]{2,1,0:T(8,128)}, f32[4,64,128]{2,1,0:T(8,128)}, u32[]{:S(2)}, u32[]{:S(2)}) collective-permute-start(f32[4,64,128]{2,1,0:T(8,128)} %bitcast.15), channel_id=1, source_target_pairs={{0,1},{1,2},{2,3},{3,4},{4,5},{5,6},{6,7},{7,8},{8,9},{9,10},{10,1... | collective-permute-start | bytes 393224 | tf_op jit(solution)/shard_map/ppermute | solution.py:17
  35.9 1.9 collective-permute-start.2
  37.8 40.3 %gather_fusion = f32[4096]{0:T(1024)} fusion(f32[65536]{0:T(1024)S(1)} %bitcast.164, s32[4096]{0:T(1024)S(1)} %broadcast_clamp_fusion), kind=kCustom, calls=%fused_computation | custom fusion | bytes 49152 | tf_op jit(solution)/shard_map/gather | solution.py:69
  78.2 0.8 squeeze.29
  78.9 1.3 dynamic-slice.21
  80.9 23.0 %gather_fusion.1 = f32[4096]{0:T(1024)S(1)} fusion(f32[65536]{0:T(1024)S(1)} %fusion.155, s32[4096]{0:T(1024)S(1)} %broadcast_clamp_fusion), kind=kCustom, calls=%fused_computation.1 | custom fusion | bytes 49152 | tf_op jit(solution)/shard_map/gather | solution.py:85
  104.1 0.8 copy-done.7
  104.9 1.8 multiply_add_fusion.1
  106.7 2.1 fusion.156
  108.8 23.0 %gather_fusion.2 = f32[4096]{0:T(1024)S(1)} fusion(f32[65536]{0:T(1024)S(1)} %fusion.156, s32[4096]{0:T(1024)S(1)} %broadcast_clamp_fusion), kind=kCustom, calls=%fused_computation.2 | custom fusion | bytes 49152 | tf_op jit(solution)/shard_map/gather | solution.py:85
  132.0 0.8 copy-done.9
  133.1 218.4 %all-reduce.4 = f32[2,512]{1,0:T(2,128)S(1)} all-reduce(f32[2,512]{1,0:T(2,128)S(1)} %pad_maximum_fusion.6), channel_id=2, replica_groups=mesh['shot'=8,'space'=64] {'space'}, use_global_device_ids=true, to_apply=%region_2.3.clone | all-reduce | flops 1024 | bytes 8192
  351.6 0.6 stack.16
  352.2 21.5 %all-to-all-start = ((f32[64,2,8]{2,1,0:T(2,128)}), f32[64,2,8]{2,1,0:T(2,128)S(1)}, u32[]{:S(2)}, u32[]{:S(2)}) async-start(f32[64,2,8]{2,1,0:T(2,128)} %stack.16), calls=%async_computation | async-start | bytes 131072 | tf_op jit(solution)/shard_map/all_to_all | solution.py:106
  373.9 0.6 fusion.55
  374.7 12.6 %all-to-all-done = f32[64,2,8]{2,1,0:T(2,128)S(1)} async-done(((f32[64,2,8]{2,1,0:T(2,128)}), f32[64,2,8]{2,1,0:T(2,128)S(1)}, u32[]{:S(2)}, u32[]{:S(2)}) %all-to-all-start) | async-done | bytes 4128 | tf_op jit(solution)/shard_map/all_to_all | solution.py:106
  388.8 28.4 %scatter_fusion = f32[65536]{0:T(1024)S(1)} fusion(f32[65536]{0:T(1024)S(1)} %bitcast.170, s32[4096]{0:T(1024)S(1)} %bitcast.179, f32[4096]{0:T(1024)S(1)} %get-tuple-element.57), kind=kCustom, calls=%fused_computation.3 | custom fusion | flops 4096 | bytes 65536 | tf_op jit(solution)/shard_map/scatter-add | solution.py:70
  417.2 2.4 collective-permute-start.5
  419.6 3.5 collective-permute-start.4
  423.1 1.0 collective-permute-done.5
  424.1 2.4 collective-permute-done.4
  427.1 28.4 %scatter_fusion.1 = f32[65536]{0:T(1024)S(1)} fusion(f32[65536]{0:T(1024)S(1)} %bitcast.173, s32[4096]{0:T(1024)S(1)} %bitcast.180, f32[4096]{0:T(1024)S(1)} %get-tuple-element.56), kind=kCustom, calls=%fused_computation.4 | custom fusion | flops 4096 | bytes 65536 | tf_op jit(solution)/shard_map/scatter-add | solution.py:70
  455.5 0.8 multiply_add_fusion
  456.3 45.4 %reduce-scatter.3.cloned.1.call-done = f32[8,8,128]{2,1,0:T(8,128)} async-done(((f32[8,64,128]{2,1,0:T(8,128)}), f32[8,8,128]{2,1,0:T(8,128)}) %reduce-scatter.3.cloned.1.call-update) | async-done | bytes 32784 | tf_op jit(solution)/shard_map/reduce_scatter | solution.py:117
  501.7 1.4 broadcast_multiply_fusion
  (85 shorter events, 5.1 us)
Async XLA Ops:
  7.2 1.0 copy-start.10
  8.2 13.1 %copy-start.3 = (f32[2,8,64,128]{3,2,1,0:T(8,128)}, f32[2,8,64,128]{3,2,1,0:T(8,128)S(1)}, u32[]{:S(2)}) copy-start(f32[2,8,64,128]{3,2,1,0:T(8,128)S(1)} %constant_dynamic-update-slice_fusion) | copy-start | bytes 1572868
  8.2 9.2 %copy-start.23 = (s32[1,512,8]{1,2,0:T(8,128)S(1)}, s32[1,512,8]{1,2,0:T(8,128)}, u32[]{:S(2)}) copy-start(s32[1,512,8]{1,2,0:T(8,128)} %param.21) | copy-start | bytes 49156
  8.3 13.0 %collective-permute-start.1 = (f32[2,4,64,128]{3,2,1,0:T(8,128)S(1)}, f32[2,4,64,128]{3,2,1,0:T(8,128)S(1)}, u32[]{:S(2)}, u32[]{:S(2)}) collective-permute-start(f32[2,4,64,128]{3,2,1,0:T(8,128)S(1)} %get-tuple-element.51), channel_id=1, source_target_pairs={{0,1},{1,2},{2,3},{3,4},{4,5},{5,6},{6,7},{7,8},{8,9},{9,10},{10,1... | collective-permute-start | bytes 786440 | tf_op jit(solution)/shard_map/ppermute | solution.py:17
  11.7 9.7 %collective-permute-start = (f32[2,4,64,128]{3,2,1,0:T(8,128)S(1)}, f32[2,4,64,128]{3,2,1,0:T(8,128)S(1)}, u32[]{:S(2)}, u32[]{:S(2)}) collective-permute-start(f32[2,4,64,128]{3,2,1,0:T(8,128)S(1)} %get-tuple-element.50), channel_id=1, source_target_pairs={{1,0},{2,1},{3,2},{4,3},{5,4},{6,5},{7,6},{8,7},{9,8},{10,9},{11,1... | collective-permute-start | bytes 786440 | tf_op jit(solution)/shard_map/ppermute | solution.py:19
  18.3 3.1 copy-start.19
  18.5 1.5 copy-start.24
  19.7 1.6 copy-start
  19.8 1.6 copy-start.6
  20.1 58.1 %copy-start.8 = (f32[1,512,8]{2,1,0:T(8,128)}, f32[1,512,8]{2,1,0:T(8,128)S(1)}, u32[]{:S(2)}) copy-start(f32[1,512,8]{2,1,0:T(8,128)S(1)} %copy.18) | copy-start | bytes 49156
  21.3 1.4 copy-start.15
  21.4 1.3 copy-start.17
  25.6 78.5 %collective-permute-start.3 = (f32[4,64,128]{2,1,0:T(8,128)}, f32[4,64,128]{2,1,0:T(8,128)}, u32[]{:S(2)}, u32[]{:S(2)}) collective-permute-start(f32[4,64,128]{2,1,0:T(8,128)} %bitcast.15), channel_id=1, source_target_pairs={{0,1},{1,2},{2,3},{3,4},{4,5},{5,6},{6,7},{7,8},{8,9},{9,10},{10,1... | collective-permute-start | bytes 393224 | tf_op jit(solution)/shard_map/ppermute | solution.py:17
  35.9 68.2 %collective-permute-start.2 = (f32[4,64,128]{2,1,0:T(8,128)}, f32[4,64,128]{2,1,0:T(8,128)}, u32[]{:S(2)}, u32[]{:S(2)}) collective-permute-start(f32[4,64,128]{2,1,0:T(8,128)} %bitcast.14), channel_id=1, source_target_pairs={{1,0},{2,1},{3,2},{4,3},{5,4},{6,5},{7,6},{8,7},{9,8},{10,9},{11,1... | collective-permute-start | bytes 393224 | tf_op jit(solution)/shard_map/ppermute | solution.py:19
  103.9 1.0 copy-start.7
  108.8 23.1 %copy-start.1 = (f32[65536]{0:T(1024)}, f32[65536]{0:T(1024)S(1)}, u32[]{:S(2)}) copy-start(f32[65536]{0:T(1024)S(1)} %fusion.156) | copy-start | bytes 786436
  108.8 23.3 %copy-start.13 = (s32[1,512,8]{2,1,0:T(8,128)S(1)}, s32[1,512,8]{2,1,0:T(8,128)}, u32[]{:S(2)}) copy-start(s32[1,512,8]{2,1,0:T(8,128)} %copy-done.12) | copy-start | bytes 49156
  108.8 242.7 %copy-start.27 = (f32[1,2,8]{2,1,0:T(2,128)S(1)}, f32[1,2,8]{2,1,0:T(2,128)}, u32[]{:S(2)}) copy-start(f32[1,2,8]{2,1,0:T(2,128)} %param.23) | copy-start | bytes 196
  108.8 265.0 %copy-start.20 = (f32[1,8,64,128]{3,2,1,0:T(8,128)S(1)}, f32[1,8,64,128]{3,2,1,0:T(8,128)}, u32[]{:S(2)}) copy-start(f32[1,8,64,128]{3,2,1,0:T(8,128)} %param.17) | copy-start | bytes 786436
  131.8 1.0 copy-start.9
  132.8 241.0 %copy-start.4 = (f32[2,8,64,128]{3,2,1,0:T(8,128)S(1)}, f32[2,8,64,128]{3,2,1,0:T(8,128)}, u32[]{:S(2)}) copy-start(f32[2,8,64,128]{3,2,1,0:T(8,128)} %copy-done.3) | copy-start | bytes 1572868
  132.8 241.0 %copy-start.11 = (f32[1,8,64,128]{3,2,1,0:T(8,128)S(1)}, f32[1,8,64,128]{3,2,1,0:T(8,128)}, u32[]{:S(2)}) copy-start(f32[1,8,64,128]{3,2,1,0:T(8,128)} %param.18) | copy-start | bytes 786436
  132.8 241.0 %copy-start.16 = (f32[2,4,64,128]{3,2,1,0:T(8,128)S(1)}, f32[2,4,64,128]{3,2,1,0:T(8,128)}, u32[]{:S(2)}) copy-start(f32[2,4,64,128]{3,2,1,0:T(8,128)} %copy-done.15) | copy-start | bytes 786436
  132.8 241.0 %copy-start.18 = (f32[2,4,64,128]{3,2,1,0:T(8,128)S(1)}, f32[2,4,64,128]{3,2,1,0:T(8,128)}, u32[]{:S(2)}) copy-start(f32[2,4,64,128]{3,2,1,0:T(8,128)} %copy-done.17) | copy-start | bytes 786436
  352.2 35.0 %all-to-all-start = ((f32[64,2,8]{2,1,0:T(2,128)}), f32[64,2,8]{2,1,0:T(2,128)S(1)}, u32[]{:S(2)}, u32[]{:S(2)}) async-start(f32[64,2,8]{2,1,0:T(2,128)} %stack.16), calls=%async_computation | async-start | bytes 131072 | tf_op jit(solution)/shard_map/all_to_all | solution.py:106
  373.8 127.9 %reduce-scatter.3.cloned.1.call-start = ((), (), s32[]{:S(2)}) async-start(), calls=%async_computation.2 | async-start | bytes 294912 | tf_op jit(solution)/shard_map/reduce_scatter | solution.py:117
  373.8 14.9 %copy-start.21 = (s32[4096,1]{0,1:T(1,128)S(1)}, s32[4096,1]{0,1:T(1,128)}, u32[]{:S(2)}) copy-start(s32[4096,1]{0,1:T(1,128)} %compare_select_fusion.1) | copy-start | bytes 49156
  388.0 0.7 copy-start.22
  417.2 6.9 %collective-permute-start.5 = (f32[4,64,128]{2,1,0:T(8,128)S(1)}, f32[4,64,128]{2,1,0:T(8,128)S(1)}, u32[]{:S(2)}, u32[]{:S(2)}) collective-permute-start(f32[4,64,128]{2,1,0:T(8,128)S(1)} %bitcast.182), channel_id=1, source_target_pairs={{0,1},{1,2},{2,3},{3,4},{4,5},{5,6},{6,7},{7,8},{8,9},{9,10},{10,1... | collective-permute-start | bytes 393224 | tf_op jit(solution)/shard_map/ppermute | solution.py:17
  419.6 6.9 %collective-permute-start.4 = (f32[4,64,128]{2,1,0:T(8,128)S(1)}, f32[4,64,128]{2,1,0:T(8,128)S(1)}, u32[]{:S(2)}, u32[]{:S(2)}) collective-permute-start(f32[4,64,128]{2,1,0:T(8,128)S(1)} %bitcast.181), channel_id=1, source_target_pairs={{1,0},{2,1},{3,2},{4,3},{5,4},{6,5},{7,6},{8,7},{9,8},{10,9},{11,1... | collective-permute-start | bytes 393224 | tf_op jit(solution)/shard_map/ppermute | solution.py:19
  427.1 28.4 %copy-start.14 = (f32[8,64,128]{2,1,0:T(8,128)S(1)}, f32[8,64,128]{2,1,0:T(8,128)}, u32[]{:S(2)}) copy-start(f32[8,64,128]{2,1,0:T(8,128)} %get-tuple-element.49) | copy-start | bytes 786436
  455.5 0.8 copy-start.2
  (4 other events, 2.7 us)
Sparse Core Ops, SparseCore 0:
  456.4 45.2 reduce-scatter.2
